TPU v7x, 32 devices: a whole 2x2x4 slice. The times are simulated.
32 devices in a mesh: rows: 8 (over y, x, core), bands: 4 (over z).
Axes of the slice: x: 2, y: 2, z: 4, core: 2. Of those that a mesh axis runs over, the one named last changes fastest.
Arguments:
- psi_panels: float32 [8192, 256], P('rows', 'bands'), may hold values from -6 to 6
- rotation: float32 [256, 8000], P('rows', 'bands'), may hold values from -0.375 to 0.375
- accumulated: float32 [8192, 8000], P('rows', 'bands'), may hold values from -6 to 6
Outputs:
- rotated: float32 [8192, 8000], P('rows', 'bands')
All inputs are finite; a program needn't handle non-finite values.
Results may differ from a plain program's by a relative error of at most 0.000059.
Values sent between devices are 32-bit elements; how exact they have to be, the bound alone decides.
A program may use at most 64 MiB of HBM per device.

v0:
```python
import jax
import jax.numpy as jnp
from jax import lax
from jax.sharding import PartitionSpec as P


def multiply(left, right):
    return jnp.dot(left, right, precision=lax.Precision.HIGHEST, preferred_element_type=jnp.float32)


def local(psi_panels, rotation, accumulated):
    psi_whole = lax.all_gather(psi_panels, "bands", axis=1, tiled=True)
    rot_whole = lax.all_gather(rotation, "rows", axis=0, tiled=True)
    rotated = accumulated + multiply(psi_whole, rot_whole)
    return rotated


def solution(mesh):
    in_specs = (P("rows", "bands"), P("rows", "bands"), P("rows", "bands"))
    out_specs = P("rows", "bands")
    return jax.shard_map(local, mesh=mesh, in_specs=in_specs, out_specs=out_specs, check_vma=False)
```

profile of v0, /device:TPU:0, one launch (start us, length us, event | category | flops | bytes accessed | tf_op | source)
XLA Modules:
  0.0 87.9 jit_solution(7715527911118243104)
XLA Ops:
  6.5 0.0 all-gather.3.cloned.1.call-start
  6.5 0.7 all-gather.3.cloned.1.call-update
  7.3 0.0 all-gather.5.cloned.1.call-start
  7.3 0.7 all-gather.5.cloned.1.call-update
  8.0 31.6 %all-gather.3.cloned.1.call-done = f32[1024,256]{0,1:T(8,128)} async-done(((f32[1024,64]{0,1:T(8,128)}), f32[1024,256]{0,1:T(8,128)}) %all-gather.3.cloned.1.call-update) | async-done | bytes 1048592 | tf_op jit(solution)/shard_map/all_gather | solution.py:12
  39.6 29.3 %all-gather.5.cloned.1.call-done = f32[256,2000]{1,0:T(8,128)} async-done(((f32[32,2000]{1,0:T(8,128)}), f32[256,2000]{1,0:T(8,128)}) %all-gather.5.cloned.1.call-update) | async-done | bytes 2048016 | tf_op jit(solution)/shard_map/all_gather | solution.py:13
  68.9 12.2 %convolution_add_fusion = f32[1024,2000]{0,1:T(8,128)} fusion(f32[1024,2000]{0,1:T(8,128)} %param.5, f32[1024,256]{0,1:T(8,128)} %all-gather.3.cloned.1.call-done, f32[256,2000]{1,0:T(8,128)} %all-gather.5.cloned.1.call-done), kind=kOutput, calls=%fused_computation | convolution fusion | flops 6293504000 | bytes 19480576 | tf_op jit(solution)/shard_map/dot_general | solution.py:8
Async XLA Ops:
  6.5 33.1 %all-gather.3.cloned.1.call-start = ((), (), s32[]{:S(2)}) async-start(), calls=%async_computation | async-start | bytes 1310720 | tf_op jit(solution)/shard_map/all_gather | solution.py:12
  7.3 61.6 %all-gather.5.cloned.1.call-start = ((), (), s32[]{:S(2)}) async-start(), calls=%async_computation.1 | async-start | bytes 2359296 | tf_op jit(solution)/shard_map/all_gather | solution.py:13
Sparse Core Ops, SparseCore 0:
  8.9 30.6 all-gather.2
  41.5 27.3 all-gather.4
where the time goes:
time: 88 us; the launch traced here: 87.9 us
  waiting for transfers between devices  62.3 us (71%)
  between operations  13.4 us (15%)
  matrix products  12.2 us (14%)
    all_gather x1, waiting for transfers between devices, local(): psi_whole = lax.all_gather(psi_panels, 'bands', axis=1, tiled=True)  31.6 us
    all_gather x1, waiting for transfers between devices, local(): rot_whole = lax.all_gather(rotation, 'rows', axis=0, tiled=True)  29.3 us
    dot_general x1, matrix products, multiply(): jnp.dot(left, right, precision=lax.Precision.HIGHEST, preferred_element_t...  12.2 us
  transfers between devices with their start and end apart: 2, of which 2 were waited for; matrix products, arithmetic and copies ran while one was open for 0% of the time, Pallas kernels for 0%

commit v1 on v0

v1 whole, which is shorter than its diff:
```python
import functools

import jax
import jax.numpy as jnp
from jax import lax
from jax.experimental import pallas as pl
from jax.experimental.pallas import tpu as pltpu
from jax.sharding import PartitionSpec as P

MESH = pl.DeviceIdType.MESH
CHUNK = 256


def split(x):
    high = x.astype(jnp.bfloat16)
    low = (x - high.astype(jnp.float32)).astype(jnp.bfloat16)
    return high, low


def kernel(n_rows, n_bands, psi_ref, rot_ref, acc_ref, out_ref,
           psi_all, rot_all, rot_split,
           psi_recv, psi_send, rot_recv, peer_send, twin_send, local_sem):
    r = lax.axis_index("rows")
    z = lax.axis_index("bands")
    n_chips = n_rows // 2
    chip, core = r // 2, r % 2
    twin = 2 * chip + 1 - core
    kz, mrows = psi_ref.shape
    kr, nb = rot_ref.shape
    chunks = mrows // CHUNK

    def peer(d):
        return 2 * lax.rem(chip + d, n_chips) + core

    def columns(c):
        return pl.ds(pl.multiple_of(c * CHUNK, CHUNK), CHUNK)

    load_acc = pltpu.make_async_copy(acc_ref, out_ref, local_sem.at[0])
    load_psi = pltpu.make_async_copy(psi_ref, psi_all.at[z], local_sem.at[1])
    load_rot = pltpu.make_async_copy(rot_ref, rot_all.at[r], local_sem.at[2])

    barrier = pltpu.get_barrier_semaphore()

    def greet(rows, bands):
        pl.semaphore_signal(barrier, inc=1, device_id=(rows, bands), device_id_type=MESH)

    pl.when(z > 0)(lambda: greet(r, z - 1))
    pl.when(z < n_bands - 1)(lambda: greet(r, z + 1))
    greet(twin, z)

    @pl.loop(1, n_chips)
    def _(d):
        greet(peer(d), z)

    expected = n_chips + jnp.where(z > 0, 1, 0) + jnp.where(z < n_bands - 1, 1, 0)
    pl.semaphore_wait(barrier, expected)

    def psi_copy(source, c, way, own=False):
        here = psi_ref if own else psi_all.at[source]
        target = z + 2 * way - 1
        return pltpu.make_async_remote_copy(
            src_ref=here.at[:, columns(c)],
            dst_ref=psi_all.at[source, :, columns(c)],
            send_sem=psi_send.at[way, source, c],
            recv_sem=psi_recv.at[source, c],
            device_id=(r, target), device_id_type=MESH)

    def rot_copy(source, target, send_sem, own=False):
        return pltpu.make_async_remote_copy(
            src_ref=rot_ref if own else rot_all.at[source],
            dst_ref=rot_all.at[source],
            send_sem=send_sem, recv_sem=rot_recv.at[source],
            device_id=(target, z), device_id_type=MESH)

    @pl.loop(0, chunks)
    def _(c):
        pl.when(z > 0)(lambda: psi_copy(z, c, 0, own=True).start())
        pl.when(z < n_bands - 1)(lambda: psi_copy(z, c, 1, own=True).start())

    @pl.loop(1, n_chips)
    def _(d):
        rot_copy(r, peer(d), peer_send.at[d], own=True).start()

    rot_copy(r, twin, twin_send.at[0], own=True).start()
    load_psi.start()
    load_rot.start()
    load_acc.start()

    if n_bands > 2:
        @pl.loop(1, n_bands - 1)
        def _(h):
            @pl.loop(0, chunks)
            def _(c):
                @pl.when((z - h >= 0) & (z + 1 < n_bands))
                def _():
                    copy = psi_copy(z - h, c, 1)
                    copy.wait_recv()
                    copy.start()

                @pl.when((z + h < n_bands) & (z > 0))
                def _():
                    copy = psi_copy(z + h, c, 0)
                    copy.wait_recv()
                    copy.start()

    @pl.loop(1, n_chips)
    def _(d):
        source = peer(n_chips - d)
        copy = rot_copy(source, twin, twin_send.at[d])
        copy.wait_recv()
        copy.start()

    @pl.loop(0, n_chips)
    def _(d):
        source = 2 * lax.rem(chip + d, n_chips) + 1 - core
        rot_copy(source, twin, twin_send.at[d]).wait_recv()

    load_rot.wait()
    for start in range(0, nb, 128):
        width = min(128, nb - start)
        block = rot_all[:, :, start:start + width].reshape(n_rows * kr, width).T
        high, low = split(block)
        rot_split[start:start + width, :] = jnp.concatenate([high, low, high], axis=1)

    load_psi.wait()
    load_acc.wait()

    @pl.loop(0, chunks)
    def _(c):
        @pl.when(z == 0)
        def _():
            @pl.loop(1, n_bands)
            def _(source):
                psi_copy(source, c, 1).wait_recv()

        @pl.when(z == n_bands - 1)
        def _():
            @pl.loop(0, n_bands - 1)
            def _(source):
                psi_copy(source, c, 0).wait_recv()

        high, low = split(psi_all[:, :, columns(c)].reshape(n_bands * kz, CHUNK))
        operand = jnp.concatenate([high, high, low], axis=0)
        out_ref[:, columns(c)] += jnp.dot(
            rot_split[...], operand, preferred_element_type=jnp.float32)

    @pl.loop(0, chunks)
    def _(c):
        @pl.when(z < n_bands - 1)
        def _():
            @pl.loop(0, z + 1)
            def _(source):
                psi_copy(source, c, 1).wait_send()

        @pl.when(z > 0)
        def _():
            @pl.loop(z, n_bands)
            def _(source):
                psi_copy(source, c, 0).wait_send()

    @pl.loop(1, n_chips)
    def _(d):
        rot_copy(r, peer(d), peer_send.at[d]).wait_send()

    @pl.loop(0, n_chips)
    def _(d):
        rot_copy(r, twin, twin_send.at[d]).wait_send()


def local(n_rows, n_bands, psi_panels, rotation, accumulated):
    psi, acc = psi_panels.T, accumulated.T
    kz, mrows = psi.shape
    kr, nb = rotation.shape
    chunks = mrows // CHUNK
    out = pl.pallas_call(
        functools.partial(kernel, n_rows, n_bands),
        out_shape=pltpu.VMEM((nb, mrows), jnp.float32),
        in_specs=[pl.BlockSpec(memory_space=pltpu.HBM)] * 3,
        out_specs=pl.BlockSpec(memory_space=pltpu.VMEM),
        scratch_shapes=[
            pltpu.VMEM((n_bands, kz, mrows), jnp.float32),
            pltpu.VMEM((n_rows, kr, nb), jnp.float32),
            pltpu.VMEM((nb, 3 * n_rows * kr), jnp.bfloat16),
            pltpu.SemaphoreType.DMA((n_bands, chunks)),
            pltpu.SemaphoreType.DMA((2, n_bands, chunks)),
            pltpu.SemaphoreType.DMA((n_rows,)),
            pltpu.SemaphoreType.DMA((n_rows // 2,)),
            pltpu.SemaphoreType.DMA((n_rows // 2,)),
            pltpu.SemaphoreType.DMA((3,)),
        ],
        compiler_params=pltpu.CompilerParams(
            collective_id=0, has_side_effects=True, vmem_limit_bytes=32 * 1024 * 1024),
        cost_estimate=pl.CostEstimate(
            flops=6 * nb * mrows * n_rows * kr, bytes_accessed=8 * nb * mrows, transcendentals=0),
        name="rotate",
    )(*(pltpu.with_memory_space_constraint(x, pltpu.HBM) for x in (psi, rotation, acc)))
    return out.T


def solution(mesh):
    sizes = mesh.shape["rows"], mesh.shape["bands"]
    specs = P("rows", "bands")
    return jax.shard_map(
        functools.partial(local, *sizes), mesh=mesh, in_specs=(specs,) * 3, out_specs=specs, check_vma=False)
```

time: 88 us -> 28.6 us (0.33)
  waiting for transfers between devices: 62.3 us -> 0 us
  Pallas kernels: 0 us -> 25.1 us
  between operations: 13.4 us -> 0.01 us
  matrix products: 12.2 us -> 0 us
  local copies, waits for them, and re-layouts: 0 us -> 3.33 us
    all_gather x2 -> x0, waiting for transfers between devices: 60.9 us -> none  [the longest x1 31.6 us: local(): psi_whole = lax.all_gather(psi_panels, 'bands', axis=1, tiled=True)]
    pallas_call x0 -> x1, Pallas kernels: none -> 25.1 us  [local(): pl.pallas_call(functools.partial(kernel, n_rows, n_bands), out_shape=pltp...]
    dot_general x1 -> x0, matrix products: 12.2 us -> none  [multiply(): jnp.dot(left, right, precision=lax.Precision.HIGHEST, preferred_element_t...]
    unnamed x0 -> x1, local copies, waits for them, and re-layouts: none -> 3.33 us
    unnamed x2 -> x0, waiting for transfers between devices: 1.41 us -> none
  transfers between devices with their start and end apart: 2 -> 0, of which waited for: 2 -> 0; matrix products, arithmetic and copies ran while one was open for 0% -> 0% of each run, Pallas kernels for 0% -> 0%
where the time goes in v1:
time: 28.6 us; the launch traced here: 28.4 us
  Pallas kernels  25.1 us (88%)
  local copies, waits for them, and re-layouts  3.33 us (12%)
    pallas_call x1, Pallas kernels, local(): pl.pallas_call(functools.partial(kernel, n_rows, n_bands), out_shape=pltp...  25.1 us
    unnamed x1, local copies, waits for them, and re-layouts  3.33 us

profile of v1, /device:TPU:0, one launch (start us, length us, event | category | flops | bytes accessed | tf_op | source)
XLA Modules:
  0.0 28.4 jit_solution(13268481099967321683)
XLA Ops:
  0.0 25.1 %rotate.1 = f32[2000,1024]{1,0:T(8,128)S(1)} custom-call(f32[64,1024]{1,0:T(8,128)} %bitcast.5, f32[32,2000]{1,0:T(8,128)} %rot_ref.1, f32[2000,1024]{1,0:T(8,128)} %bitcast.4), custom_call_target="tpu_custom_call" | custom-call | flops 3145728000 | bytes 16384000 | tf_op jit(solution)/shard_map/rotate/pallas_call | solution.py:175
  25.1 3.3 %copy.5 = f32[1024,2000]{0,1:T(8,128)} copy(f32[1024,2000]{0,1:T(8,128)S(1)} %bitcast.3) | data formatting | bytes 16384000

commit v2 on v1

--- a/solution.py
+++ b/solution.py
@@ -15,6 +15,10 @@
     high = x.astype(jnp.bfloat16)
     low = (x - high.astype(jnp.float32)).astype(jnp.bfloat16)
     return high, low
+
+
+def parts_of(n_rows):
+    return 2 if n_rows == 8 else 1
 
 
 def kernel(n_rows, n_bands, psi_ref, rot_ref, acc_ref, out_ref,
@@ -28,6 +32,12 @@
     kz, mrows = psi_ref.shape
     kr, nb = rot_ref.shape
     chunks = mrows // CHUNK
+    square = n_chips == 4
+    parts = parts_of(n_rows)
+    x, y = chip % 2, chip // 2
+    xn = 2 * (2 * y + 1 - x) + core
+    yn = 2 * (2 * (1 - y) + x) + core
+    dn = 2 * (2 * (1 - y) + 1 - x) + core
 
     def peer(d):
         return 2 * lax.rem(chip + d, n_chips) + core
@@ -65,55 +75,91 @@
             recv_sem=psi_recv.at[source, c],
             device_id=(r, target), device_id_type=MESH)
 
-    def rot_copy(source, target, send_sem, own=False):
+    def rot_copy(source, part, target, send_sem, own=False):
+        here = rot_ref if own else rot_all.at[source]
+        rows = pl.ds(part * (kr // parts), kr // parts)
         return pltpu.make_async_remote_copy(
-            src_ref=rot_ref if own else rot_all.at[source],
-            dst_ref=rot_all.at[source],
-            send_sem=send_sem, recv_sem=rot_recv.at[source],
+            src_ref=here.at[rows],
+            dst_ref=rot_all.at[source, rows],
+            send_sem=send_sem, recv_sem=rot_recv.at[source, part],
             device_id=(target, z), device_id_type=MESH)
 
-    @pl.loop(0, chunks)
-    def _(c):
+    def own_psi(c):
         pl.when(z > 0)(lambda: psi_copy(z, c, 0, own=True).start())
         pl.when(z < n_bands - 1)(lambda: psi_copy(z, c, 1, own=True).start())
 
-    @pl.loop(1, n_chips)
-    def _(d):
-        rot_copy(r, peer(d), peer_send.at[d], own=True).start()
-
-    rot_copy(r, twin, twin_send.at[0], own=True).start()
+    def own_psi_sent(c):
+        pl.when(z > 0)(lambda: psi_copy(z, c, 0, own=True).wait_send())
+        pl.when(z < n_bands - 1)(lambda: psi_copy(z, c, 1, own=True).wait_send())
+
+    def pass_on(h, c):
+        @pl.when((z - h >= 0) & (z + 1 < n_bands))
+        def _():
+            copy = psi_copy(z - h, c, 1)
+            copy.wait_recv()
+            copy.start()
+
+        @pl.when((z + h < n_bands) & (z > 0))
+        def _():
+            copy = psi_copy(z + h, c, 0)
+            copy.wait_recv()
+            copy.start()
+
+    def to_twin(source, part, d, wait=True):
+        copy = rot_copy(source, part, twin, twin_send.at[d, part], own=not wait)
+        if wait:
+            copy.wait_recv()
+        copy.start()
+
+    for c in range(min(2, chunks)):
+        own_psi(c)
+
+    if square:
+        sends = [(xn, 0, 1), (yn, 1, 2), (xn, 1, 1), (yn, 0, 2)]
+        for target, part, d in sends:
+            rot_copy(r, part, target, peer_send.at[d, part], own=True).start()
+    else:
+        @pl.loop(1, n_chips)
+        def _(d):
+            rot_copy(r, 0, peer(d), peer_send.at[d, 0], own=True).start()
+    for part in range(parts):
+        to_twin(r, part, 0, wait=False)
     load_psi.start()
     load_rot.start()
     load_acc.start()
 
+    @pl.loop(2, chunks)
+    def _(c):
+        own_psi_sent(c - 2)
+        own_psi(c)
+
+    if n_bands > 3:
+        @pl.loop(1, n_bands - 2)
+        def _(h):
+            pl.loop(0, chunks)(lambda c: pass_on(h, c))
+
+    if square:
+        for source, part, target, d in ((xn, 0, yn, 1), (yn, 1, xn, 2)):
+            to_twin(source, part, d)
+            rot_copy(source, part, target, peer_send.at[0, part]).start()
+        to_twin(xn, 1, 1)
+        to_twin(yn, 0, 2)
+        for part in range(parts):
+            to_twin(dn, part, 3)
+    else:
+        @pl.loop(1, n_chips)
+        def _(d):
+            to_twin(peer(n_chips - d), 0, d)
+
     if n_bands > 2:
-        @pl.loop(1, n_bands - 1)
-        def _(h):
-            @pl.loop(0, chunks)
-            def _(c):
-                @pl.when((z - h >= 0) & (z + 1 < n_bands))
-                def _():
-                    copy = psi_copy(z - h, c, 1)
-                    copy.wait_recv()
-                    copy.start()
-
-                @pl.when((z + h < n_bands) & (z > 0))
-                def _():
-                    copy = psi_copy(z + h, c, 0)
-                    copy.wait_recv()
-                    copy.start()
-
-    @pl.loop(1, n_chips)
-    def _(d):
-        source = peer(n_chips - d)
-        copy = rot_copy(source, twin, twin_send.at[d])
-        copy.wait_recv()
-        copy.start()
+        for c in range(min(2, chunks)):
+            pass_on(n_bands - 2, c)
 
     @pl.loop(0, n_chips)
     def _(d):
         source = 2 * lax.rem(chip + d, n_chips) + 1 - core
-        rot_copy(source, twin, twin_send.at[d]).wait_recv()
+        for part in range(parts):
+            rot_copy(source, part, twin, twin_send.at[d, part]).wait_recv()
 
     load_rot.wait()
     for start in range(0, nb, 128):
@@ -127,6 +173,9 @@
 
     @pl.loop(0, chunks)
     def _(c):
+        if n_bands > 2:
+            pl.when(c + 2 < chunks)(lambda: pass_on(n_bands - 2, c + 2))
+
         @pl.when(z == 0)
         def _():
             @pl.loop(1, n_bands)
@@ -144,27 +193,34 @@
         out_ref[:, columns(c)] += jnp.dot(
             rot_split[...], operand, preferred_element_type=jnp.float32)
 
+    pl.loop(max(0, chunks - 2), chunks)(own_psi_sent)
+
     @pl.loop(0, chunks)
     def _(c):
         @pl.when(z < n_bands - 1)
         def _():
-            @pl.loop(0, z + 1)
+            @pl.loop(0, z)
             def _(source):
                 psi_copy(source, c, 1).wait_send()
 
         @pl.when(z > 0)
         def _():
-            @pl.loop(z, n_bands)
+            @pl.loop(z + 1, n_bands)
             def _(source):
                 psi_copy(source, c, 0).wait_send()
 
-    @pl.loop(1, n_chips)
-    def _(d):
-        rot_copy(r, peer(d), peer_send.at[d]).wait_send()
+    if square:
+        for target, part, d in sends + [(yn, 0, 0), (xn, 1, 0)]:
+            rot_copy(r, part, target, peer_send.at[d, part]).wait_send()
+    else:
+        @pl.loop(1, n_chips)
+        def _(d):
+            rot_copy(r, 0, peer(d), peer_send.at[d, 0]).wait_send()
 
     @pl.loop(0, n_chips)
     def _(d):
-        rot_copy(r, twin, twin_send.at[d]).wait_send()
+        for part in range(parts):
+            rot_copy(r, part, twin, twin_send.at[d, part]).wait_send()
 
 
 def local(n_rows, n_bands, psi_panels, rotation, accumulated):
@@ -183,9 +239,9 @@
             pltpu.VMEM((nb, 3 * n_rows * kr), jnp.bfloat16),
             pltpu.SemaphoreType.DMA((n_bands, chunks)),
             pltpu.SemaphoreType.DMA((2, n_bands, chunks)),
-            pltpu.SemaphoreType.DMA((n_rows,)),
-            pltpu.SemaphoreType.DMA((n_rows // 2,)),
-            pltpu.SemaphoreType.DMA((n_rows // 2,)),
+            pltpu.SemaphoreType.DMA((n_rows, parts_of(n_rows))),
+            pltpu.SemaphoreType.DMA((n_rows // 2, parts_of(n_rows))),
+            pltpu.SemaphoreType.DMA((n_rows // 2, parts_of(n_rows))),
             pltpu.SemaphoreType.DMA((3,)),
         ],
         compiler_params=pltpu.CompilerParams(

time: 28.6 us -> 29.1 us (1.017)
  Pallas kernels: 25.1 us -> 25.6 us
    pallas_call x1, Pallas kernels: 25.1 us -> 25.6 us  [local(): pl.pallas_call(functools.partial(kernel, n_rows, n_bands), out_shape=pltp...]
where the time goes in v2:
time: 29.1 us; the launch traced here: 29 us
  Pallas kernels  25.6 us (88%)
  local copies, waits for them, and re-layouts  3.33 us (11%)
    pallas_call x1, Pallas kernels, local(): pl.pallas_call(functools.partial(kernel, n_rows, n_bands), out_shape=pltp...  25.6 us
    unnamed x1, local copies, waits for them, and re-layouts  3.33 us

profile of v2, /device:TPU:0, one launch (start us, length us, event | category | flops | bytes accessed | tf_op | source)
XLA Modules:
  0.0 29.0 jit_solution(10180312278808648966)
XLA Ops:
  0.0 25.6 %rotate.1 = f32[2000,1024]{1,0:T(8,128)S(1)} custom-call(f32[64,1024]{1,0:T(8,128)} %bitcast.5, f32[32,2000]{1,0:T(8,128)} %rot_ref.1, f32[2000,1024]{1,0:T(8,128)} %bitcast.4), custom_call_target="tpu_custom_call" | custom-call | flops 3145728000 | bytes 16384000 | tf_op jit(solution)/shard_map/rotate/pallas_call | solution.py:231
  25.6 3.3 %copy.5 = f32[1024,2000]{0,1:T(8,128)} copy(f32[1024,2000]{0,1:T(8,128)S(1)} %bitcast.3) | data formatting | bytes 16384000

commit v3 on v2

--- a/solution.py
+++ b/solution.py
@@ -17,12 +17,22 @@
     return high, low
 
 
+def rot_operand(block):
+    high, low = split(block.T)
+    return jnp.concatenate([high, low, high, low], axis=1)
+
+
+def psi_operand(block):
+    high, low = split(block)
+    return jnp.concatenate([high, high, low, low], axis=0)
+
+
 def parts_of(n_rows):
     return 2 if n_rows == 8 else 1
 
 
-def kernel(n_rows, n_bands, psi_ref, rot_ref, acc_ref, out_ref,
-           psi_all, rot_all, rot_split,
+def kernel(n_rows, n_bands, psi_ref, rot_ref, acc_ref, out_ref, rot_late, psi_late,
+           psi_all, rot_all, rot_early,
            psi_recv, psi_send, rot_recv, peer_send, twin_send, local_sem):
     r = lax.axis_index("rows")
     z = lax.axis_index("bands")
@@ -161,12 +171,20 @@
         for part in range(parts):
             rot_copy(source, part, twin, twin_send.at[d, part]).wait_recv()
 
+    far_down = 2 * z >= n_bands
+    late = jnp.where(far_down, 0, n_bands - 1)
+    first = jnp.where(far_down, 1, 0)
+    inward = jnp.where(far_down, 0, 1)
+    per_band = n_rows // n_bands
+
     load_rot.wait()
     for start in range(0, nb, 128):
         width = min(128, nb - start)
-        block = rot_all[:, :, start:start + width].reshape(n_rows * kr, width).T
-        high, low = split(block)
-        rot_split[start:start + width, :] = jnp.concatenate([high, low, high], axis=1)
+        columns_here = slice(start, start + width)
+        early = rot_all[pl.ds(first * per_band, n_rows - per_band), :, columns_here]
+        rot_early[columns_here, :] = rot_operand(early.reshape(-1, width))
+        last = rot_all[pl.ds(late * per_band, per_band), :, columns_here]
+        rot_late[columns_here, :] = rot_operand(last.reshape(-1, width))
 
     load_psi.wait()
     load_acc.wait()
@@ -176,22 +194,23 @@
         if n_bands > 2:
             pl.when(c + 2 < chunks)(lambda: pass_on(n_bands - 2, c + 2))
 
-        @pl.when(z == 0)
-        def _():
-            @pl.loop(1, n_bands)
+        @pl.when((z == 0) | (z == n_bands - 1))
+        def _():
+            @pl.loop(1, n_bands - 1)
             def _(source):
-                psi_copy(source, c, 1).wait_recv()
-
-        @pl.when(z == n_bands - 1)
-        def _():
-            @pl.loop(0, n_bands - 1)
-            def _(source):
-                psi_copy(source, c, 0).wait_recv()
-
-        high, low = split(psi_all[:, :, columns(c)].reshape(n_bands * kz, CHUNK))
-        operand = jnp.concatenate([high, high, low], axis=0)
+                psi_copy(source, c, inward).wait_recv()
+
+        early = psi_all[pl.ds(first, n_bands - 1), :, columns(c)]
         out_ref[:, columns(c)] += jnp.dot(
-            rot_split[...], operand, preferred_element_type=jnp.float32)
+            rot_early[...], psi_operand(early.reshape(-1, CHUNK)), preferred_element_type=jnp.float32)
+
+    @pl.loop(0, chunks)
+    def _(c):
+        @pl.when((z == 0) | (z == n_bands - 1))
+        def _():
+            psi_copy(late, c, inward).wait_recv()
+
+        psi_late[:, columns(c)] = psi_operand(psi_all[late, :, columns(c)])
 
     pl.loop(max(0, chunks - 2), chunks)(own_psi_sent)
 
@@ -223,33 +242,66 @@
             rot_copy(r, part, twin, twin_send.at[d, part]).wait_send()
 
 
+def finish(sum_ref, rot_ref, psi_ref, out_ref, held, sems):
+    copies = []
+    for c in range(held.shape[0]):
+        columns = pl.ds(c * CHUNK, CHUNK)
+        held[c] = sum_ref[:, columns] + jnp.dot(
+            rot_ref[...], psi_ref[:, columns], preferred_element_type=jnp.float32)
+        copies.append(pltpu.make_async_copy(held.at[c], out_ref.at[:, columns], sems.at[c]))
+        copies[-1].start()
+    for copy in copies:
+        copy.wait()
+
+
 def local(n_rows, n_bands, psi_panels, rotation, accumulated):
     psi, acc = psi_panels.T, accumulated.T
     kz, mrows = psi.shape
     kr, nb = rotation.shape
     chunks = mrows // CHUNK
-    out = pl.pallas_call(
+    parts = parts_of(n_rows)
+    vmem, hbm = pl.BlockSpec(memory_space=pltpu.VMEM), pl.BlockSpec(memory_space=pltpu.HBM)
+    mib = 1024 * 1024
+    partial = pl.pallas_call(
         functools.partial(kernel, n_rows, n_bands),
-        out_shape=pltpu.VMEM((nb, mrows), jnp.float32),
-        in_specs=[pl.BlockSpec(memory_space=pltpu.HBM)] * 3,
-        out_specs=pl.BlockSpec(memory_space=pltpu.VMEM),
+        out_shape=[
+            pltpu.VMEM((nb, mrows), jnp.float32),
+            pltpu.VMEM((nb, 4 * kz), jnp.bfloat16),
+            pltpu.VMEM((4 * kz, mrows), jnp.bfloat16),
+        ],
+        in_specs=[hbm] * 3,
+        out_specs=[vmem] * 3,
         scratch_shapes=[
             pltpu.VMEM((n_bands, kz, mrows), jnp.float32),
             pltpu.VMEM((n_rows, kr, nb), jnp.float32),
-            pltpu.VMEM((nb, 3 * n_rows * kr), jnp.bfloat16),
+            pltpu.VMEM((nb, 4 * (n_bands - 1) * kz), jnp.bfloat16),
             pltpu.SemaphoreType.DMA((n_bands, chunks)),
             pltpu.SemaphoreType.DMA((2, n_bands, chunks)),
-            pltpu.SemaphoreType.DMA((n_rows, parts_of(n_rows))),
-            pltpu.SemaphoreType.DMA((n_rows // 2, parts_of(n_rows))),
-            pltpu.SemaphoreType.DMA((n_rows // 2, parts_of(n_rows))),
+            pltpu.SemaphoreType.DMA((n_rows, parts)),
+            pltpu.SemaphoreType.DMA((n_rows // 2, parts)),
+            pltpu.SemaphoreType.DMA((n_rows // 2, parts)),
             pltpu.SemaphoreType.DMA((3,)),
         ],
         compiler_params=pltpu.CompilerParams(
-            collective_id=0, has_side_effects=True, vmem_limit_bytes=32 * 1024 * 1024),
+            collective_id=0, has_side_effects=True, vmem_limit_bytes=24 * mib),
         cost_estimate=pl.CostEstimate(
-            flops=6 * nb * mrows * n_rows * kr, bytes_accessed=8 * nb * mrows, transcendentals=0),
+            flops=6 * nb * mrows * n_rows * kr, bytes_accessed=4 * nb * mrows, transcendentals=0),
         name="rotate",
     )(*(pltpu.with_memory_space_constraint(x, pltpu.HBM) for x in (psi, rotation, acc)))
+    out = pl.pallas_call(
+        finish,
+        out_shape=jax.ShapeDtypeStruct((nb, mrows), jnp.float32),
+        in_specs=[vmem] * 3,
+        out_specs=hbm,
+        scratch_shapes=[
+            pltpu.VMEM((chunks, nb, CHUNK), jnp.float32),
+            pltpu.SemaphoreType.DMA((chunks,)),
+        ],
+        compiler_params=pltpu.CompilerParams(vmem_limit_bytes=24 * mib),
+        cost_estimate=pl.CostEstimate(
+            flops=8 * nb * mrows * kz, bytes_accessed=4 * nb * mrows, transcendentals=0),
+        name="finish",
+    )(*(pltpu.with_memory_space_constraint(x, pltpu.VMEM) for x in partial))
     return out.T
 
 

time: 29.1 us -> 28.6 us (0.983)
  local copies, waits for them, and re-layouts: 3.33 us -> 0 us
  Pallas kernels: 25.6 us -> 28.4 us
    unnamed x1 -> x0, local copies, waits for them, and re-layouts: 3.33 us -> none
    pallas_call x1 -> x2, Pallas kernels: 25.6 us -> 28.4 us  [the longest x1 24.3 us: local(): pl.pallas_call(functools.partial(kernel, n_rows, n_bands), out_shape=[plt...]
where the time goes in v3:
time: 28.6 us; the launch traced here: 28.4 us
  Pallas kernels  28.4 us (99%)
    pallas_call x1, Pallas kernels, local(): pl.pallas_call(functools.partial(kernel, n_rows, n_bands), out_shape=[plt...  24.3 us
    pallas_call x1, Pallas kernels, local(): pl.pallas_call(finish, out_shape=jax.ShapeDtypeStruct((nb, mrows), jnp.fl...  4.19 us

profile of v3, /device:TPU:0, one launch (start us, length us, event | category | flops | bytes accessed | tf_op | source)
XLA Modules:
  0.0 28.4 jit_solution(3196488599670948677)
XLA Ops:
  0.0 24.3 %rotate.1 = (f32[2000,1024]{1,0:T(8,128)S(1)}, bf16[2000,256]{1,0:T(8,128)(2,1)S(1)}, bf16[256,1024]{1,0:T(8,128)(2,1)S(1)}) custom-call(f32[64,1024]{1,0:T(8,128)} %bitcast.4, f32[32,2000]{1,0:T(8,128)} %rot_ref.1, f32[2000,1024]{1,0:T(8,128)} %bitcast.3), custom_call_target="tpu_custom_call" | custom-call | flops 3145728000 | bytes 8192000 | tf_op jit(solution)/shard_map/rotate/pallas_call | solution.py:265
  24.3 4.2 %finish.1 = f32[2000,1024]{1,0:T(8,128)} custom-call(f32[2000,1024]{1,0:T(8,128)S(1)} %get-tuple-element.8.sum_ref, bf16[2000,256]{1,0:T(8,128)(2,1)S(1)} %get-tuple-element.9.rot_ref, bf16[256,1024]{1,0:T(8,128)(2,1)S(1)} %get-tuple-element.10.psi_ref), custom_call_target="tpu_custom_call" | custom-call | flops 1048576000 | bytes 8192000 | tf_op jit(solution)/shard_map/finish/pallas_call | solution.py:291

commit v4 on v3

--- a/solution.py
+++ b/solution.py
@@ -9,6 +9,7 @@
 
 MESH = pl.DeviceIdType.MESH
 CHUNK = 256
+WIDE = 512
 
 
 def split(x):
@@ -17,6 +18,11 @@
     return high, low
 
 
+def block_rows(nb):
+    fit = [rows for rows in range(16, 513, 16) if nb % rows == 0]
+    return max(fit, default=nb)
+
+
 def rot_operand(block):
     high, low = split(block.T)
     return jnp.concatenate([high, low, high, low], axis=1)
@@ -32,7 +38,7 @@
 
 
 def kernel(n_rows, n_bands, psi_ref, rot_ref, acc_ref, out_ref, rot_late, psi_late,
-           psi_all, rot_all, rot_early,
+           psi_all, rot_all, rot_early, psi_early,
            psi_recv, psi_send, rot_recv, peer_send, twin_send, local_sem):
     r = lax.axis_index("rows")
     z = lax.axis_index("bands")
@@ -178,31 +184,56 @@
     per_band = n_rows // n_bands
 
     load_rot.wait()
-    for start in range(0, nb, 128):
-        width = min(128, nb - start)
-        columns_here = slice(start, start + width)
-        early = rot_all[pl.ds(first * per_band, n_rows - per_band), :, columns_here]
-        rot_early[columns_here, :] = rot_operand(early.reshape(-1, width))
-        last = rot_all[pl.ds(late * per_band, per_band), :, columns_here]
-        rot_late[columns_here, :] = rot_operand(last.reshape(-1, width))
+
+    def make_operands(start, width):
+        here = pl.ds(start, width)
+        early = rot_all[pl.ds(first * per_band, n_rows - per_band), :, here]
+        rot_early[here, :] = rot_operand(early.reshape(-1, width))
+        last = rot_all[pl.ds(late * per_band, per_band), :, here]
+        rot_late[here, :] = rot_operand(last.reshape(-1, width))
+
+    @pl.loop(0, nb // 128)
+    def _(i):
+        make_operands(pl.multiple_of(i * 128, 128), 128)
+
+    if nb % 128:
+        make_operands(nb // 128 * 128, nb % 128)
 
     load_psi.wait()
     load_acc.wait()
 
-    @pl.loop(0, chunks)
-    def _(c):
-        if n_bands > 2:
-            pl.when(c + 2 < chunks)(lambda: pass_on(n_bands - 2, c + 2))
+    tall = block_rows(nb)
+    blocks = nb // tall
+    halves = mrows // WIDE
+    per_half = WIDE // CHUNK
+
+    @pl.loop(0, halves)
+    def _(half):
+        wide = pl.ds(pl.multiple_of(half * WIDE, WIDE), WIDE)
 
         @pl.when((z == 0) | (z == n_bands - 1))
         def _():
             @pl.loop(1, n_bands - 1)
             def _(source):
-                psi_copy(source, c, inward).wait_recv()
-
-        early = psi_all[pl.ds(first, n_bands - 1), :, columns(c)]
-        out_ref[:, columns(c)] += jnp.dot(
-            rot_early[...], psi_operand(early.reshape(-1, CHUNK)), preferred_element_type=jnp.float32)
+                for c in range(per_half):
+                    psi_copy(source, half * per_half + c, inward).wait_recv()
+
+        early = psi_all[pl.ds(first, n_bands - 1), :, wide]
+        psi_early[...] = psi_operand(early.reshape(-1, WIDE))
+
+        @pl.loop(0, blocks)
+        def _(block):
+            turn = half * blocks + block
+            c = 2 + turn // 3
+            if n_bands > 2:
+                pl.when((turn % 3 == 0) & (c < chunks))(lambda: pass_on(n_bands - 2, c))
+            rows = pl.ds(pl.multiple_of(block * tall, tall), tall)
+            out_ref[rows, wide] += jnp.dot(
+                rot_early[rows, :], psi_early[...], preferred_element_type=jnp.float32)
+
+    if n_bands > 2:
+        for c in range(2 + pl.cdiv(halves * blocks, 3), chunks):
+            pass_on(n_bands - 2, c)
 
     @pl.loop(0, chunks)
     def _(c):
@@ -243,15 +274,20 @@
 
 
 def finish(sum_ref, rot_ref, psi_ref, out_ref, held, sems):
-    copies = []
-    for c in range(held.shape[0]):
-        columns = pl.ds(c * CHUNK, CHUNK)
-        held[c] = sum_ref[:, columns] + jnp.dot(
-            rot_ref[...], psi_ref[:, columns], preferred_element_type=jnp.float32)
-        copies.append(pltpu.make_async_copy(held.at[c], out_ref.at[:, columns], sems.at[c]))
-        copies[-1].start()
-    for copy in copies:
-        copy.wait()
+    blocks, tall, _ = held.shape
+
+    def write(block):
+        rows = pl.ds(pl.multiple_of(block * tall, tall), tall)
+        return pltpu.make_async_copy(held.at[block], out_ref.at[rows], sems.at[block])
+
+    @pl.loop(0, blocks)
+    def _(block):
+        rows = pl.ds(pl.multiple_of(block * tall, tall), tall)
+        held[block] = sum_ref[rows, :] + jnp.dot(
+            rot_ref[rows, :], psi_ref[...], preferred_element_type=jnp.float32)
+        write(block).start()
+
+    pl.loop(0, blocks)(lambda block: write(block).wait())
 
 
 def local(n_rows, n_bands, psi_panels, rotation, accumulated):
@@ -260,6 +296,7 @@
     kr, nb = rotation.shape
     chunks = mrows // CHUNK
     parts = parts_of(n_rows)
+    tall = block_rows(nb)
     vmem, hbm = pl.BlockSpec(memory_space=pltpu.VMEM), pl.BlockSpec(memory_space=pltpu.HBM)
     mib = 1024 * 1024
     partial = pl.pallas_call(
@@ -275,6 +312,7 @@
             pltpu.VMEM((n_bands, kz, mrows), jnp.float32),
             pltpu.VMEM((n_rows, kr, nb), jnp.float32),
             pltpu.VMEM((nb, 4 * (n_bands - 1) * kz), jnp.bfloat16),
+            pltpu.VMEM((4 * (n_bands - 1) * kz, WIDE), jnp.bfloat16),
             pltpu.SemaphoreType.DMA((n_bands, chunks)),
             pltpu.SemaphoreType.DMA((2, n_bands, chunks)),
             pltpu.SemaphoreType.DMA((n_rows, parts)),
@@ -294,8 +332,8 @@
         in_specs=[vmem] * 3,
         out_specs=hbm,
         scratch_shapes=[
-            pltpu.VMEM((chunks, nb, CHUNK), jnp.float32),
-            pltpu.SemaphoreType.DMA((chunks,)),
+            pltpu.VMEM((nb // tall, tall, mrows), jnp.float32),
+            pltpu.SemaphoreType.DMA((nb // tall,)),
         ],
         compiler_params=pltpu.CompilerParams(vmem_limit_bytes=24 * mib),
         cost_estimate=pl.CostEstimate(

time: 28.6 us -> 30.4 us (1.063)
  Pallas kernels: 28.4 us -> 30.1 us
    pallas_call x1, Pallas kernels: 24.3 us -> 26.4 us  [local(): pl.pallas_call(functools.partial(kernel, n_rows, n_bands), out_shape=[plt...]
    pallas_call x1, Pallas kernels: 4.19 us -> 3.7 us  [local(): pl.pallas_call(finish, out_shape=jax.ShapeDtypeStruct((nb, mrows), jnp.fl...]
where the time goes in v4:
time: 30.4 us; the launch traced here: 30.1 us
  Pallas kernels  30.1 us (99%)
    pallas_call x1, Pallas kernels, local(): pl.pallas_call(functools.partial(kernel, n_rows, n_bands), out_shape=[plt...  26.4 us
    pallas_call x1, Pallas kernels, local(): pl.pallas_call(finish, out_shape=jax.ShapeDtypeStruct((nb, mrows), jnp.fl...  3.7 us

profile of v4, /device:TPU:0, one launch (start us, length us, event | category | flops | bytes accessed | tf_op | source)
XLA Modules:
  0.0 30.1 jit_solution(9518774654579501921)
XLA Ops:
  0.0 26.4 %rotate.1 = (f32[2000,1024]{1,0:T(8,128)S(1)}, bf16[2000,256]{1,0:T(8,128)(2,1)S(1)}, bf16[256,1024]{1,0:T(8,128)(2,1)S(1)}) custom-call(f32[64,1024]{1,0:T(8,128)} %bitcast.4, f32[32,2000]{1,0:T(8,128)} %rot_ref.1, f32[2000,1024]{1,0:T(8,128)} %bitcast.3), custom_call_target="tpu_custom_call" | custom-call | flops 3145728000 | bytes 8192000 | tf_op jit(solution)/shard_map/rotate/pallas_call | solution.py:302
  26.4 3.7 %finish.1 = f32[2000,1024]{1,0:T(8,128)} custom-call(f32[2000,1024]{1,0:T(8,128)S(1)} %get-tuple-element.8.sum_ref, bf16[2000,256]{1,0:T(8,128)(2,1)S(1)} %get-tuple-element.9.rot_ref, bf16[256,1024]{1,0:T(8,128)(2,1)S(1)} %get-tuple-element.10.psi_ref), custom_call_target="tpu_custom_call" | custom-call | flops 1048576000 | bytes 8192000 | tf_op jit(solution)/shard_map/finish/pallas_call | solution.py:329

commit v5 on v4

--- a/solution.py
+++ b/solution.py
@@ -9,7 +9,6 @@
 
 MESH = pl.DeviceIdType.MESH
 CHUNK = 256
-WIDE = 512
 
 
 def split(x):
@@ -24,8 +23,9 @@
 
 
 def rot_operand(block):
-    high, low = split(block.T)
-    return jnp.concatenate([high, low, high, low], axis=1)
+    high = block.astype(jnp.bfloat16).astype(jnp.float32)
+    both = jnp.concatenate([high, block - high], axis=0).T.astype(jnp.bfloat16)
+    return jnp.concatenate([both, both], axis=1)
 
 
 def psi_operand(block):
@@ -37,8 +37,8 @@
     return 2 if n_rows == 8 else 1
 
 
-def kernel(n_rows, n_bands, psi_ref, rot_ref, acc_ref, out_ref, rot_late, psi_late,
-           psi_all, rot_all, rot_early, psi_early,
+def kernel(n_rows, n_bands, psi_ref, rot_ref, acc_ref, out_ref, rot_op, psi_late,
+           psi_all, rot_all, psi_early,
            psi_recv, psi_send, rot_recv, peer_send, twin_send, local_sem):
     r = lax.axis_index("rows")
     z = lax.axis_index("bands")
@@ -149,98 +149,113 @@
         own_psi_sent(c - 2)
         own_psi(c)
 
+    def make_operand(s):
+        def columns_from(start, width):
+            here = pl.ds(start, width)
+            block = rot_all[pl.ds(2 * s, 2), :, here].reshape(kz, width)
+            rot_op[s, here, :] = rot_operand(block)
+
+        full = nb // 128
+        group = 5 if full % 5 == 0 else 1
+
+        @pl.loop(0, full // group)
+        def _(i):
+            for j in range(group):
+                columns_from(pl.multiple_of((i * group + j) * 128, 128), 128)
+
+        if nb % 128:
+            columns_from(full * 128, nb % 128)
+
+    def from_twin(s):
+        for part in range(parts):
+            rot_copy(2 * s + 1 - core, part, twin, twin_send.at[0, part]).wait_recv()
+
+    load_rot.wait()
+    from_twin(chip)
+    make_operand(chip)
+
+    last_hop = n_bands - 2
     if n_bands > 3:
-        @pl.loop(1, n_bands - 2)
-        def _(h):
-            pl.loop(0, chunks)(lambda c: pass_on(h, c))
-
+        for c in range(min(2, chunks)):
+            pass_on(1, c)
     if square:
         for source, part, target, d in ((xn, 0, yn, 1), (yn, 1, xn, 2)):
             to_twin(source, part, d)
             rot_copy(source, part, target, peer_send.at[0, part]).start()
+    if n_bands > 3:
+        for c in range(2, chunks):
+            pass_on(1, c)
+
+        @pl.loop(2, last_hop)
+        def _(h):
+            pl.loop(0, chunks)(lambda c: pass_on(h, c))
+
+    if square:
         to_twin(xn, 1, 1)
         to_twin(yn, 0, 2)
+        for s in (xn // 2, yn // 2):
+            from_twin(s)
+            make_operand(s)
+        if n_bands > 2:
+            for c in range(min(2, chunks)):
+                pass_on(last_hop, c)
         for part in range(parts):
             to_twin(dn, part, 3)
+        from_twin(dn // 2)
+        make_operand(dn // 2)
     else:
         @pl.loop(1, n_chips)
         def _(d):
             to_twin(peer(n_chips - d), 0, d)
 
-    if n_bands > 2:
-        for c in range(min(2, chunks)):
-            pass_on(n_bands - 2, c)
-
-    @pl.loop(0, n_chips)
-    def _(d):
-        source = 2 * lax.rem(chip + d, n_chips) + 1 - core
-        for part in range(parts):
-            rot_copy(source, part, twin, twin_send.at[d, part]).wait_recv()
+        if n_bands > 2:
+            for c in range(min(2, chunks)):
+                pass_on(last_hop, c)
+
+        @pl.loop(1, n_chips)
+        def _(d):
+            s = lax.rem(chip + d, n_chips)
+            from_twin(s)
+            make_operand(s)
 
     far_down = 2 * z >= n_bands
     late = jnp.where(far_down, 0, n_bands - 1)
     first = jnp.where(far_down, 1, 0)
     inward = jnp.where(far_down, 0, 1)
-    per_band = n_rows // n_bands
-
-    load_rot.wait()
-
-    def make_operands(start, width):
-        here = pl.ds(start, width)
-        early = rot_all[pl.ds(first * per_band, n_rows - per_band), :, here]
-        rot_early[here, :] = rot_operand(early.reshape(-1, width))
-        last = rot_all[pl.ds(late * per_band, per_band), :, here]
-        rot_late[here, :] = rot_operand(last.reshape(-1, width))
-
-    @pl.loop(0, nb // 128)
-    def _(i):
-        make_operands(pl.multiple_of(i * 128, 128), 128)
-
-    if nb % 128:
-        make_operands(nb // 128 * 128, nb % 128)
+    at_end = (z == 0) | (z == n_bands - 1)
 
     load_psi.wait()
+
+    @pl.when(at_end)
+    def _():
+        @pl.loop(1, n_bands - 1)
+        def _(source):
+            pl.loop(0, chunks)(lambda c: psi_copy(source, c, inward).wait_recv())
+
+    @pl.loop(0, n_bands - 1)
+    def _(j):
+        psi_early[j] = psi_operand(psi_all[first + j])
+
     load_acc.wait()
-
     tall = block_rows(nb)
     blocks = nb // tall
-    halves = mrows // WIDE
-    per_half = WIDE // CHUNK
-
-    @pl.loop(0, halves)
-    def _(half):
-        wide = pl.ds(pl.multiple_of(half * WIDE, WIDE), WIDE)
-
-        @pl.when((z == 0) | (z == n_bands - 1))
-        def _():
-            @pl.loop(1, n_bands - 1)
-            def _(source):
-                for c in range(per_half):
-                    psi_copy(source, half * per_half + c, inward).wait_recv()
-
-        early = psi_all[pl.ds(first, n_bands - 1), :, wide]
-        psi_early[...] = psi_operand(early.reshape(-1, WIDE))
-
-        @pl.loop(0, blocks)
-        def _(block):
-            turn = half * blocks + block
-            c = 2 + turn // 3
-            if n_bands > 2:
-                pl.when((turn % 3 == 0) & (c < chunks))(lambda: pass_on(n_bands - 2, c))
-            rows = pl.ds(pl.multiple_of(block * tall, tall), tall)
-            out_ref[rows, wide] += jnp.dot(
-                rot_early[rows, :], psi_early[...], preferred_element_type=jnp.float32)
+
+    @pl.loop(0, blocks)
+    def _(block):
+        if n_bands > 2:
+            pl.when(block + 2 < chunks)(lambda: pass_on(last_hop, block + 2))
+        rows = pl.ds(pl.multiple_of(block * tall, tall), tall)
+        left = jnp.concatenate([rot_op[first + j, rows, :] for j in range(n_bands - 1)], axis=1)
+        out_ref[rows, :] += jnp.dot(
+            left, psi_early[...].reshape(-1, mrows), preferred_element_type=jnp.float32)
 
     if n_bands > 2:
-        for c in range(2 + pl.cdiv(halves * blocks, 3), chunks):
-            pass_on(n_bands - 2, c)
+        for c in range(2 + blocks, chunks):
+            pass_on(last_hop, c)
 
     @pl.loop(0, chunks)
     def _(c):
-        @pl.when((z == 0) | (z == n_bands - 1))
-        def _():
-            psi_copy(late, c, inward).wait_recv()
-
+        pl.when(at_end)(lambda: psi_copy(late, c, inward).wait_recv())
         psi_late[:, columns(c)] = psi_operand(psi_all[late, :, columns(c)])
 
     pl.loop(max(0, chunks - 2), chunks)(own_psi_sent)
@@ -273,8 +288,9 @@
             rot_copy(r, part, twin, twin_send.at[d, part]).wait_send()
 
 
-def finish(sum_ref, rot_ref, psi_ref, out_ref, held, sems):
+def finish(n_bands, sum_ref, rot_ref, psi_ref, out_ref, held, sems):
     blocks, tall, _ = held.shape
+    late = jnp.where(2 * lax.axis_index("bands") >= n_bands, 0, n_bands - 1)
 
     def write(block):
         rows = pl.ds(pl.multiple_of(block * tall, tall), tall)
@@ -284,7 +300,7 @@
     def _(block):
         rows = pl.ds(pl.multiple_of(block * tall, tall), tall)
         held[block] = sum_ref[rows, :] + jnp.dot(
-            rot_ref[rows, :], psi_ref[...], preferred_element_type=jnp.float32)
+            rot_ref[late, rows, :], psi_ref[...], preferred_element_type=jnp.float32)
         write(block).start()
 
     pl.loop(0, blocks)(lambda block: write(block).wait())
@@ -303,7 +319,7 @@
         functools.partial(kernel, n_rows, n_bands),
         out_shape=[
             pltpu.VMEM((nb, mrows), jnp.float32),
-            pltpu.VMEM((nb, 4 * kz), jnp.bfloat16),
+            pltpu.VMEM((n_bands, nb, 4 * kz), jnp.bfloat16),
             pltpu.VMEM((4 * kz, mrows), jnp.bfloat16),
         ],
         in_specs=[hbm] * 3,
@@ -311,8 +327,7 @@
         scratch_shapes=[
             pltpu.VMEM((n_bands, kz, mrows), jnp.float32),
             pltpu.VMEM((n_rows, kr, nb), jnp.float32),
-            pltpu.VMEM((nb, 4 * (n_bands - 1) * kz), jnp.bfloat16),
-            pltpu.VMEM((4 * (n_bands - 1) * kz, WIDE), jnp.bfloat16),
+            pltpu.VMEM((n_bands - 1, 4 * kz, mrows), jnp.bfloat16),
             pltpu.SemaphoreType.DMA((n_bands, chunks)),
             pltpu.SemaphoreType.DMA((2, n_bands, chunks)),
             pltpu.SemaphoreType.DMA((n_rows, parts)),
@@ -327,7 +342,7 @@
         name="rotate",
     )(*(pltpu.with_memory_space_constraint(x, pltpu.HBM) for x in (psi, rotation, acc)))
     out = pl.pallas_call(
-        finish,
+        functools.partial(finish, n_bands),
         out_shape=jax.ShapeDtypeStruct((nb, mrows), jnp.float32),
         in_specs=[vmem] * 3,
         out_specs=hbm,

time: 30.4 us -> 27.6 us (0.908)
  Pallas kernels: 30.1 us -> 27.4 us
    pallas_call x1, Pallas kernels: 26.4 us -> 23.7 us  [local(): pl.pallas_call(functools.partial(kernel, n_rows, n_bands), out_shape=[plt...]
where the time goes in v5:
time: 27.6 us; the launch traced here: 27.5 us
  Pallas kernels  27.4 us (99%)
    pallas_call x1, Pallas kernels, local(): pl.pallas_call(functools.partial(kernel, n_rows, n_bands), out_shape=[plt...  23.7 us
    pallas_call x1, Pallas kernels, local(): pl.pallas_call(functools.partial(finish, n_bands), out_shape=jax.ShapeDty...  3.72 us

profile of v5, /device:TPU:0, one launch (start us, length us, event | category | flops | bytes accessed | tf_op | source)
XLA Modules:
  0.0 27.5 jit_solution(16903388945506442934)
XLA Ops:
  0.0 23.7 %rotate.1 = (f32[2000,1024]{1,0:T(8,128)S(1)}, bf16[4,2000,256]{2,1,0:T(8,128)(2,1)S(1)}, bf16[256,1024]{1,0:T(8,128)(2,1)S(1)}) custom-call(f32[64,1024]{1,0:T(8,128)} %bitcast.4, f32[32,2000]{1,0:T(8,128)} %rot_ref.1, f32[2000,1024]{1,0:T(8,128)} %bitcast.3), custom_call_target="tpu_custom_call" | custom-call | flops 3145728000 | bytes 8192000 | tf_op jit(solution)/shard_map/rotate/pallas_call | solution.py:318
  23.7 3.7 %finish.1 = f32[2000,1024]{1,0:T(8,128)} custom-call(f32[2000,1024]{1,0:T(8,128)S(1)} %get-tuple-element.8.sum_ref, bf16[4,2000,256]{2,1,0:T(8,128)(2,1)S(1)} %get-tuple-element.9.rot_ref, bf16[256,1024]{1,0:T(8,128)(2,1)S(1)} %get-tuple-element.10.psi_ref), custom_call_target="tpu_custom_call" | custom-call | flops 1048576000 | bytes 8192000 | tf_op jit(solution)/shard_map/finish/pallas_call | solution.py:344

commit v6 on v5

--- a/solution.py
+++ b/solution.py
@@ -8,13 +8,16 @@
 from jax.sharding import PartitionSpec as P
 
 MESH = pl.DeviceIdType.MESH
-CHUNK = 256
 
 
 def split(x):
     high = x.astype(jnp.bfloat16)
     low = (x - high.astype(jnp.float32)).astype(jnp.bfloat16)
     return high, low
+
+
+def chunks_of(kz):
+    return max(n for n in (1, 2, 4) if kz % (8 * n) == 0)
 
 
 def block_rows(nb):
@@ -47,7 +50,7 @@
     twin = 2 * chip + 1 - core
     kz, mrows = psi_ref.shape
     kr, nb = rot_ref.shape
-    chunks = mrows // CHUNK
+    chunks = chunks_of(kz)
     square = n_chips == 4
     parts = parts_of(n_rows)
     x, y = chip % 2, chip // 2
@@ -58,8 +61,8 @@
     def peer(d):
         return 2 * lax.rem(chip + d, n_chips) + core
 
-    def columns(c):
-        return pl.ds(pl.multiple_of(c * CHUNK, CHUNK), CHUNK)
+    def panel_rows(c):
+        return pl.ds(pl.multiple_of(c * (kz // chunks), kz // chunks), kz // chunks)
 
     load_acc = pltpu.make_async_copy(acc_ref, out_ref, local_sem.at[0])
     load_psi = pltpu.make_async_copy(psi_ref, psi_all.at[z], local_sem.at[1])
@@ -85,8 +88,8 @@
         here = psi_ref if own else psi_all.at[source]
         target = z + 2 * way - 1
         return pltpu.make_async_remote_copy(
-            src_ref=here.at[:, columns(c)],
-            dst_ref=psi_all.at[source, :, columns(c)],
+            src_ref=here.at[panel_rows(c)],
+            dst_ref=psi_all.at[source, panel_rows(c)],
             send_sem=psi_send.at[way, source, c],
             recv_sem=psi_recv.at[source, c],
             device_id=(r, target), device_id_type=MESH)
@@ -190,23 +193,72 @@
         def _(h):
             pl.loop(0, chunks)(lambda c: pass_on(h, c))
 
-    if square:
+    far_down = 2 * z >= n_bands
+    late = jnp.where(far_down, 0, n_bands - 1)
+    first = jnp.where(far_down, 1, 0)
+    inward = jnp.where(far_down, 0, 1)
+    at_end = (z == 0) | (z == n_bands - 1)
+    tall = block_rows(nb)
+    blocks = nb // tall
+
+    def arrived(source):
+        pl.loop(0, chunks)(lambda c: psi_copy(source, c, inward).wait_recv())
+
+    def add_products(sources, meanwhile):
+        n = len(sources)
+        for j, source in enumerate(sources):
+            psi_early[j] = psi_operand(psi_all[source])
+
+        @pl.loop(0, blocks)
+        def _(block):
+            meanwhile(block)
+            rows = pl.ds(pl.multiple_of(block * tall, tall), tall)
+            left = jnp.concatenate([rot_op[source, rows, :] for source in sources], axis=1)
+            out_ref[rows, :] += jnp.dot(
+                left, psi_early[0:n].reshape(-1, mrows), preferred_element_type=jnp.float32)
+
+    def last_hop_at(block):
+        if n_bands > 2:
+            pl.when(block + 2 < chunks)(lambda: pass_on(last_hop, block + 2))
+
+    if square and n_bands > 3:
         to_twin(xn, 1, 1)
         to_twin(yn, 0, 2)
         for s in (xn // 2, yn // 2):
             from_twin(s)
             make_operand(s)
-        if n_bands > 2:
-            for c in range(min(2, chunks)):
+        load_psi.wait()
+        load_acc.wait()
+        inner = jnp.where(far_down, z - 1, z + 1)
+        soon = jnp.where(z == dn // 2, inner, z)
+        pl.when(at_end)(lambda: arrived(inner))
+
+        def first_two(block):
+            pl.when(block == 0)(lambda: pass_on(last_hop, 0))
+            pl.when(block == 2)(lambda: pass_on(last_hop, 1))
+
+        add_products([soon], first_two)
+        for c in (0, 1):
+            if 2 * c >= blocks:
                 pass_on(last_hop, c)
         for part in range(parts):
             to_twin(dn, part, 3)
+
+        @pl.when(at_end)
+        def _():
+            @pl.loop(0, n_bands - 3)
+            def _(j):
+                arrived(j + 2 - first)
+
         from_twin(dn // 2)
         make_operand(dn // 2)
+        rest = [first + j + jnp.where(first + j >= soon, 1, 0) for j in range(n_bands - 2)]
     else:
         @pl.loop(1, n_chips)
         def _(d):
-            to_twin(peer(n_chips - d), 0, d)
+            source = peer(n_chips - d)
+            for part in range(parts):
+                to_twin(source, part, d)
 
         if n_bands > 2:
             for c in range(min(2, chunks)):
@@ -218,45 +270,22 @@
             from_twin(s)
             make_operand(s)
 
-    far_down = 2 * z >= n_bands
-    late = jnp.where(far_down, 0, n_bands - 1)
-    first = jnp.where(far_down, 1, 0)
-    inward = jnp.where(far_down, 0, 1)
-    at_end = (z == 0) | (z == n_bands - 1)
-
-    load_psi.wait()
-
-    @pl.when(at_end)
-    def _():
-        @pl.loop(1, n_bands - 1)
-        def _(source):
-            pl.loop(0, chunks)(lambda c: psi_copy(source, c, inward).wait_recv())
-
-    @pl.loop(0, n_bands - 1)
-    def _(j):
-        psi_early[j] = psi_operand(psi_all[first + j])
-
-    load_acc.wait()
-    tall = block_rows(nb)
-    blocks = nb // tall
-
-    @pl.loop(0, blocks)
-    def _(block):
-        if n_bands > 2:
-            pl.when(block + 2 < chunks)(lambda: pass_on(last_hop, block + 2))
-        rows = pl.ds(pl.multiple_of(block * tall, tall), tall)
-        left = jnp.concatenate([rot_op[first + j, rows, :] for j in range(n_bands - 1)], axis=1)
-        out_ref[rows, :] += jnp.dot(
-            left, psi_early[...].reshape(-1, mrows), preferred_element_type=jnp.float32)
-
+        load_psi.wait()
+        load_acc.wait()
+
+        @pl.when(at_end)
+        def _():
+            pl.loop(1, n_bands - 1)(arrived)
+
+        rest = [first + j for j in range(n_bands - 1)]
+
+    add_products(rest, last_hop_at)
     if n_bands > 2:
         for c in range(2 + blocks, chunks):
             pass_on(last_hop, c)
 
-    @pl.loop(0, chunks)
-    def _(c):
-        pl.when(at_end)(lambda: psi_copy(late, c, inward).wait_recv())
-        psi_late[:, columns(c)] = psi_operand(psi_all[late, :, columns(c)])
+    pl.when(at_end)(lambda: arrived(late))
+    psi_late[...] = psi_operand(psi_all[late])
 
     pl.loop(max(0, chunks - 2), chunks)(own_psi_sent)
 
@@ -310,7 +339,7 @@
     psi, acc = psi_panels.T, accumulated.T
     kz, mrows = psi.shape
     kr, nb = rotation.shape
-    chunks = mrows // CHUNK
+    chunks = chunks_of(kz)
     parts = parts_of(n_rows)
     tall = block_rows(nb)
     vmem, hbm = pl.BlockSpec(memory_space=pltpu.VMEM), pl.BlockSpec(memory_space=pltpu.HBM)

time: 27.6 us -> 29.1 us (1.054)
  Pallas kernels: 27.4 us -> 29 us
    pallas_call x1, Pallas kernels: 23.7 us -> 25.3 us  [local(): pl.pallas_call(functools.partial(kernel, n_rows, n_bands), out_shape=[plt...]
where the time goes in v6:
time: 29.1 us; the launch traced here: 29 us
  Pallas kernels  29 us (100%)
    pallas_call x1, Pallas kernels, local(): pl.pallas_call(functools.partial(kernel, n_rows, n_bands), out_shape=[plt...  25.3 us
    pallas_call x1, Pallas kernels, local(): pl.pallas_call(functools.partial(finish, n_bands), out_shape=jax.ShapeDty...  3.72 us

profile of v6, /device:TPU:0, one launch (start us, length us, event | category | flops | bytes accessed | tf_op | source)
XLA Modules:
  0.0 29.0 jit_solution(16978821528152403879)
XLA Ops:
  0.0 25.3 %rotate.1 = (f32[2000,1024]{1,0:T(8,128)S(1)}, bf16[4,2000,256]{2,1,0:T(8,128)(2,1)S(1)}, bf16[256,1024]{1,0:T(8,128)(2,1)S(1)}) custom-call(f32[64,1024]{1,0:T(8,128)} %bitcast.4, f32[32,2000]{1,0:T(8,128)} %rot_ref.1, f32[2000,1024]{1,0:T(8,128)} %bitcast.3), custom_call_target="tpu_custom_call" | custom-call | flops 3145728000 | bytes 8192000 | tf_op jit(solution)/shard_map/rotate/pallas_call | solution.py:347
  25.3 3.7 %finish.1 = f32[2000,1024]{1,0:T(8,128)} custom-call(f32[2000,1024]{1,0:T(8,128)S(1)} %get-tuple-element.8.sum_ref, bf16[4,2000,256]{2,1,0:T(8,128)(2,1)S(1)} %get-tuple-element.9.rot_ref, bf16[256,1024]{1,0:T(8,128)(2,1)S(1)} %get-tuple-element.10.psi_ref), custom_call_target="tpu_custom_call" | custom-call | flops 1048576000 | bytes 8192000 | tf_op jit(solution)/shard_map/finish/pallas_call | solution.py:373

commit v7 on v5

--- a/solution.py
+++ b/solution.py
@@ -219,8 +219,8 @@
             make_operand(s)
 
     far_down = 2 * z >= n_bands
-    late = jnp.where(far_down, 0, n_bands - 1)
-    first = jnp.where(far_down, 1, 0)
+    late = jnp.where(far_down, 0, n_bands - 2)
+    first = jnp.where(far_down, 2, 0)
     inward = jnp.where(far_down, 0, 1)
     at_end = (z == 0) | (z == n_bands - 1)
 
@@ -228,11 +228,12 @@
 
     @pl.when(at_end)
     def _():
-        @pl.loop(1, n_bands - 1)
-        def _(source):
+        @pl.loop(1, n_bands - 2)
+        def _(j):
+            source = j + first // 2
             pl.loop(0, chunks)(lambda c: psi_copy(source, c, inward).wait_recv())
 
-    @pl.loop(0, n_bands - 1)
+    @pl.loop(0, n_bands - 2)
     def _(j):
         psi_early[j] = psi_operand(psi_all[first + j])
 
@@ -245,7 +246,7 @@
         if n_bands > 2:
             pl.when(block + 2 < chunks)(lambda: pass_on(last_hop, block + 2))
         rows = pl.ds(pl.multiple_of(block * tall, tall), tall)
-        left = jnp.concatenate([rot_op[first + j, rows, :] for j in range(n_bands - 1)], axis=1)
+        left = jnp.concatenate([rot_op[first + j, rows, :] for j in range(n_bands - 2)], axis=1)
         out_ref[rows, :] += jnp.dot(
             left, psi_early[...].reshape(-1, mrows), preferred_element_type=jnp.float32)
 
@@ -253,10 +254,12 @@
         for c in range(2 + blocks, chunks):
             pass_on(last_hop, c)
 
-    @pl.loop(0, chunks)
-    def _(c):
-        pl.when(at_end)(lambda: psi_copy(late, c, inward).wait_recv())
-        psi_late[:, columns(c)] = psi_operand(psi_all[late, :, columns(c)])
+    for j in range(2):
+        @pl.when(at_end)
+        def _():
+            pl.loop(0, chunks)(lambda c: psi_copy(late + j, c, inward).wait_recv())
+
+        psi_late[j] = psi_operand(psi_all[late + j])
 
     pl.loop(max(0, chunks - 2), chunks)(own_psi_sent)
 
@@ -290,7 +293,7 @@
 
 def finish(n_bands, sum_ref, rot_ref, psi_ref, out_ref, held, sems):
     blocks, tall, _ = held.shape
-    late = jnp.where(2 * lax.axis_index("bands") >= n_bands, 0, n_bands - 1)
+    late = jnp.where(2 * lax.axis_index("bands") >= n_bands, 0, n_bands - 2)
 
     def write(block):
         rows = pl.ds(pl.multiple_of(block * tall, tall), tall)
@@ -299,8 +302,9 @@
     @pl.loop(0, blocks)
     def _(block):
         rows = pl.ds(pl.multiple_of(block * tall, tall), tall)
-        held[block] = sum_ref[rows, :] + jnp.dot(
-            rot_ref[late, rows, :], psi_ref[...], preferred_element_type=jnp.float32)
+        left = jnp.concatenate([rot_ref[late, rows, :], rot_ref[late + 1, rows, :]], axis=1)
+        right = psi_ref[...].reshape(-1, psi_ref.shape[2])
+        held[block] = sum_ref[rows, :] + jnp.dot(left, right, preferred_element_type=jnp.float32)
         write(block).start()
 
     pl.loop(0, blocks)(lambda block: write(block).wait())
@@ -320,14 +324,14 @@
         out_shape=[
             pltpu.VMEM((nb, mrows), jnp.float32),
             pltpu.VMEM((n_bands, nb, 4 * kz), jnp.bfloat16),
-            pltpu.VMEM((4 * kz, mrows), jnp.bfloat16),
+            pltpu.VMEM((2, 4 * kz, mrows), jnp.bfloat16),
         ],
         in_specs=[hbm] * 3,
         out_specs=[vmem] * 3,
         scratch_shapes=[
             pltpu.VMEM((n_bands, kz, mrows), jnp.float32),
             pltpu.VMEM((n_rows, kr, nb), jnp.float32),
-            pltpu.VMEM((n_bands - 1, 4 * kz, mrows), jnp.bfloat16),
+            pltpu.VMEM((n_bands - 2, 4 * kz, mrows), jnp.bfloat16),
             pltpu.SemaphoreType.DMA((n_bands, chunks)),
             pltpu.SemaphoreType.DMA((2, n_bands, chunks)),
             pltpu.SemaphoreType.DMA((n_rows, parts)),
@@ -352,7 +356,7 @@
         ],
         compiler_params=pltpu.CompilerParams(vmem_limit_bytes=24 * mib),
         cost_estimate=pl.CostEstimate(
-            flops=8 * nb * mrows * kz, bytes_accessed=4 * nb * mrows, transcendentals=0),
+            flops=16 * nb * mrows * kz, bytes_accessed=4 * nb * mrows, transcendentals=0),
         name="finish",
     )(*(pltpu.with_memory_space_constraint(x, pltpu.VMEM) for x in partial))
     return out.T

time: 27.6 us -> 28.2 us (1.022)
  Pallas kernels: 27.4 us -> 28 us
    pallas_call x1, Pallas kernels: 3.72 us -> 4.21 us  [local(): pl.pallas_call(functools.partial(finish, n_bands), out_shape=jax.ShapeDty...]
where the time goes in v7:
time: 28.2 us; the launch traced here: 28 us
  Pallas kernels  28 us (99%)
    pallas_call x1, Pallas kernels, local(): pl.pallas_call(functools.partial(kernel, n_rows, n_bands), out_shape=[plt...  23.8 us
    pallas_call x1, Pallas kernels, local(): pl.pallas_call(functools.partial(finish, n_bands), out_shape=jax.ShapeDty...  4.21 us

profile of v7, /device:TPU:0, one launch (start us, length us, event | category | flops | bytes accessed | tf_op | source)
XLA Modules:
  0.0 28.0 jit_solution(11918969178761903382)
XLA Ops:
  0.0 23.8 %rotate.1 = (f32[2000,1024]{1,0:T(8,128)S(1)}, bf16[4,2000,256]{2,1,0:T(8,128)(2,1)S(1)}, bf16[2,256,1024]{2,1,0:T(8,128)(2,1)S(1)}) custom-call(f32[64,1024]{1,0:T(8,128)} %bitcast.4, f32[32,2000]{1,0:T(8,128)} %rot_ref.1, f32[2000,1024]{1,0:T(8,128)} %bitcast.3), custom_call_target="tpu_custom_call" | custom-call | flops 3145728000 | bytes 8192000 | tf_op jit(solution)/shard_map/rotate/pallas_call | solution.py:322
  23.8 4.2 %finish.1 = f32[2000,1024]{1,0:T(8,128)} custom-call(f32[2000,1024]{1,0:T(8,128)S(1)} %get-tuple-element.8.sum_ref, bf16[4,2000,256]{2,1,0:T(8,128)(2,1)S(1)} %get-tuple-element.9.rot_ref, bf16[2,256,1024]{2,1,0:T(8,128)(2,1)S(1)} %get-tuple-element.10.psi_ref), custom_call_target="tpu_custom_call" | custom-call | flops 2097152000 | bytes 8192000 | tf_op jit(solution)/shard_map/finish/pallas_call | solution.py:348

commit v8 on v5

--- a/solution.py
+++ b/solution.py
@@ -288,22 +288,30 @@
             rot_copy(r, part, twin, twin_send.at[d, part]).wait_send()
 
 
-def finish(n_bands, sum_ref, rot_ref, psi_ref, out_ref, held, sems):
-    blocks, tall, _ = held.shape
+def finish(n_bands, tall, sum_ref, rot_ref, psi_ref, out_ref, held, sems):
     late = jnp.where(2 * lax.axis_index("bands") >= n_bands, 0, n_bands - 1)
-
-    def write(block):
-        rows = pl.ds(pl.multiple_of(block * tall, tall), tall)
-        return pltpu.make_async_copy(held.at[block], out_ref.at[rows], sems.at[block])
-
-    @pl.loop(0, blocks)
-    def _(block):
-        rows = pl.ds(pl.multiple_of(block * tall, tall), tall)
-        held[block] = sum_ref[rows, :] + jnp.dot(
+    blocks = held.shape[0] // tall
+    lead = [(0, tall // 5), (tall // 5, tall * 2 // 5), (tall * 3 // 5, tall * 2 // 5)]
+    if tall % 80:
+        lead = [(0, tall)]
+
+    def write(rows, i):
+        return pltpu.make_async_copy(held.at[rows], out_ref.at[rows], sems.at[i])
+
+    def add(rows, i):
+        held[rows, :] = sum_ref[rows, :] + jnp.dot(
             rot_ref[late, rows, :], psi_ref[...], preferred_element_type=jnp.float32)
-        write(block).start()
-
-    pl.loop(0, blocks)(lambda block: write(block).wait())
+        write(rows, i).start()
+
+    def block_at(block):
+        return pl.ds(pl.multiple_of(block * tall, tall), tall)
+
+    for i, (start, size) in enumerate(lead):
+        add(pl.ds(start, size), i)
+    pl.loop(1, blocks)(lambda block: add(block_at(block), block + 2))
+    for i, (start, size) in enumerate(lead):
+        write(pl.ds(start, size), i).wait()
+    pl.loop(1, blocks)(lambda block: write(block_at(block), block + 2).wait())
 
 
 def local(n_rows, n_bands, psi_panels, rotation, accumulated):
@@ -342,13 +350,13 @@
         name="rotate",
     )(*(pltpu.with_memory_space_constraint(x, pltpu.HBM) for x in (psi, rotation, acc)))
     out = pl.pallas_call(
-        functools.partial(finish, n_bands),
+        functools.partial(finish, n_bands, tall),
         out_shape=jax.ShapeDtypeStruct((nb, mrows), jnp.float32),
         in_specs=[vmem] * 3,
         out_specs=hbm,
         scratch_shapes=[
-            pltpu.VMEM((nb // tall, tall, mrows), jnp.float32),
-            pltpu.SemaphoreType.DMA((nb // tall,)),
+            pltpu.VMEM((nb, mrows), jnp.float32),
+            pltpu.SemaphoreType.DMA((nb // tall + 2,)),
         ],
         compiler_params=pltpu.CompilerParams(vmem_limit_bytes=24 * mib),
         cost_estimate=pl.CostEstimate(

time: 27.6 us -> 27.5 us (level)
  no operation moved by 1% of the time
where the time goes in v8:
time: 27.5 us; the launch traced here: 27.3 us
  Pallas kernels  27.3 us (99%)
    pallas_call x1, Pallas kernels, local(): pl.pallas_call(functools.partial(kernel, n_rows, n_bands), out_shape=[plt...  23.7 us
    pallas_call x1, Pallas kernels, local(): pl.pallas_call(functools.partial(finish, n_bands, tall), out_shape=jax.Sh...  3.61 us

profile of v8, /device:TPU:0, one launch (start us, length us, event | category | flops | bytes accessed | tf_op | source)
XLA Modules:
  0.0 27.3 jit_solution(15992013073765403440)
XLA Ops:
  0.0 23.7 %rotate.1 = (f32[2000,1024]{1,0:T(8,128)S(1)}, bf16[4,2000,256]{2,1,0:T(8,128)(2,1)S(1)}, bf16[256,1024]{1,0:T(8,128)(2,1)S(1)}) custom-call(f32[64,1024]{1,0:T(8,128)} %bitcast.4, f32[32,2000]{1,0:T(8,128)} %rot_ref.1, f32[2000,1024]{1,0:T(8,128)} %bitcast.3), custom_call_target="tpu_custom_call" | custom-call | flops 3145728000 | bytes 8192000 | tf_op jit(solution)/shard_map/rotate/pallas_call | solution.py:326
  23.7 3.6 %finish.1 = f32[2000,1024]{1,0:T(8,128)} custom-call(f32[2000,1024]{1,0:T(8,128)S(1)} %get-tuple-element.8.sum_ref, bf16[4,2000,256]{2,1,0:T(8,128)(2,1)S(1)} %get-tuple-element.9.rot_ref, bf16[256,1024]{1,0:T(8,128)(2,1)S(1)} %get-tuple-element.10.psi_ref), custom_call_target="tpu_custom_call" | custom-call | flops 1048576000 | bytes 8192000 | tf_op jit(solution)/shard_map/finish/pallas_call | solution.py:352

commit v9 on v8

--- a/solution.py
+++ b/solution.py
@@ -8,13 +8,16 @@
 from jax.sharding import PartitionSpec as P
 
 MESH = pl.DeviceIdType.MESH
-CHUNK = 256
 
 
 def split(x):
     high = x.astype(jnp.bfloat16)
     low = (x - high.astype(jnp.float32)).astype(jnp.bfloat16)
     return high, low
+
+
+def chunks_of(kz):
+    return max(n for n in (1, 2, 4) if kz % (8 * n) == 0)
 
 
 def block_rows(nb):
@@ -47,7 +50,7 @@
     twin = 2 * chip + 1 - core
     kz, mrows = psi_ref.shape
     kr, nb = rot_ref.shape
-    chunks = mrows // CHUNK
+    chunks = chunks_of(kz)
     square = n_chips == 4
     parts = parts_of(n_rows)
     x, y = chip % 2, chip // 2
@@ -58,8 +61,8 @@
     def peer(d):
         return 2 * lax.rem(chip + d, n_chips) + core
 
-    def columns(c):
-        return pl.ds(pl.multiple_of(c * CHUNK, CHUNK), CHUNK)
+    def panel_rows(c):
+        return pl.ds(pl.multiple_of(c * (kz // chunks), kz // chunks), kz // chunks)
 
     load_acc = pltpu.make_async_copy(acc_ref, out_ref, local_sem.at[0])
     load_psi = pltpu.make_async_copy(psi_ref, psi_all.at[z], local_sem.at[1])
@@ -85,8 +88,8 @@
         here = psi_ref if own else psi_all.at[source]
         target = z + 2 * way - 1
         return pltpu.make_async_remote_copy(
-            src_ref=here.at[:, columns(c)],
-            dst_ref=psi_all.at[source, :, columns(c)],
+            src_ref=here.at[panel_rows(c)],
+            dst_ref=psi_all.at[source, panel_rows(c)],
             send_sem=psi_send.at[way, source, c],
             recv_sem=psi_recv.at[source, c],
             device_id=(r, target), device_id_type=MESH)
@@ -256,7 +259,8 @@
     @pl.loop(0, chunks)
     def _(c):
         pl.when(at_end)(lambda: psi_copy(late, c, inward).wait_recv())
-        psi_late[:, columns(c)] = psi_operand(psi_all[late, :, columns(c)])
+
+    psi_late[...] = psi_operand(psi_all[late])
 
     pl.loop(max(0, chunks - 2), chunks)(own_psi_sent)
 
@@ -318,7 +322,7 @@
     psi, acc = psi_panels.T, accumulated.T
     kz, mrows = psi.shape
     kr, nb = rotation.shape
-    chunks = mrows // CHUNK
+    chunks = chunks_of(kz)
     parts = parts_of(n_rows)
     tall = block_rows(nb)
     vmem, hbm = pl.BlockSpec(memory_space=pltpu.VMEM), pl.BlockSpec(memory_space=pltpu.HBM)

time: 27.5 us -> 27.5 us (level)
  no operation moved by 1% of the time
where the time goes in v9:
time: 27.5 us; the launch traced here: 27.4 us
  Pallas kernels  27.4 us (100%)
    pallas_call x1, Pallas kernels, local(): pl.pallas_call(functools.partial(kernel, n_rows, n_bands), out_shape=[plt...  23.8 us
    pallas_call x1, Pallas kernels, local(): pl.pallas_call(functools.partial(finish, n_bands, tall), out_shape=jax.Sh...  3.61 us

profile of v9, /device:TPU:0, one launch (start us, length us, event | category | flops | bytes accessed | tf_op | source)
XLA Modules:
  0.0 27.4 jit_solution(16460231430218949078)
XLA Ops:
  0.0 23.8 %rotate.1 = (f32[2000,1024]{1,0:T(8,128)S(1)}, bf16[4,2000,256]{2,1,0:T(8,128)(2,1)S(1)}, bf16[256,1024]{1,0:T(8,128)(2,1)S(1)}) custom-call(f32[64,1024]{1,0:T(8,128)} %bitcast.4, f32[32,2000]{1,0:T(8,128)} %rot_ref.1, f32[2000,1024]{1,0:T(8,128)} %bitcast.3), custom_call_target="tpu_custom_call" | custom-call | flops 3145728000 | bytes 8192000 | tf_op jit(solution)/shard_map/rotate/pallas_call | solution.py:330
  23.8 3.6 %finish.1 = f32[2000,1024]{1,0:T(8,128)} custom-call(f32[2000,1024]{1,0:T(8,128)S(1)} %get-tuple-element.8.sum_ref, bf16[4,2000,256]{2,1,0:T(8,128)(2,1)S(1)} %get-tuple-element.9.rot_ref, bf16[256,1024]{1,0:T(8,128)(2,1)S(1)} %get-tuple-element.10.psi_ref), custom_call_target="tpu_custom_call" | custom-call | flops 1048576000 | bytes 8192000 | tf_op jit(solution)/shard_map/finish/pallas_call | solution.py:356
